TPU v7x, 32 devices: a whole 2x2x4 slice. The times are simulated.
32 devices in a mesh: groups: 2 (over y), inst: 4 (over z), dom: 4 (over x, core).
Axes of the slice: x: 2, y: 2, z: 4, core: 2. Of those that a mesh axis runs over, the one named last changes fastest.
Arguments:
- flow_state: float32 [10, 512, 512], P('groups', 'dom', 'inst'), parts along dimension 0, may hold values from -2 to 3.5, as said below
- op_weight: bfloat16 [9, 320, 320], replicated, may hold values from -0.109375 to 0.109375
- adjacency: int32 [512, 6], P('dom'), may hold values from 0 to 511, as said below
- face_tile: int32 [1024], P('dom'), may hold values from 0 to 511, as said below
- face_row: int32 [1024], P('dom'), may hold values from 0 to 63
- face_partner: int32 [1024], P('dom'), may hold values from 0 to 511
- face_side: int32 [1024], P('dom'), may hold values from 0 to 1
- face_count: int32 [4], P('dom'), may hold values from 64 to 256, as said below
- frequency: float32 [2], P('groups'), parts along dimension 0, may hold values from 0.05 to 0.2
Outputs:
- residual: float32 [10, 512, 512], P('groups', 'dom', 'inst'), parts along dimension 0
There are 2 independent parts, one for each index of `groups`. A program takes and returns all parts, laid end to end along the dimension named above; an argument that names none is the same for every part. Nothing has to cross between parts.
Inputs may be any that keep to these rules, and one draw needn't show every extreme that they name: `flow_state`: density (component 0) lies in [0.5, 2], energy (component 4) in [2, 3.5], momenta in [-2, 2]. `adjacency`: each neighbour lies within 16 tiles of its tile; upper slots point up, lower slots down, clipped at the slab's ends. `face_tile`: row n's tile lies in partition n // 256. `face_count`: at least 64; one partition uses all 256 rows in every draw.
All inputs are finite; a program needn't handle non-finite values.
Results may differ from a plain program's by a relative error of at most 0.0029.
Values may be sent and summed in bfloat16 or wider, within the bound.
A program may use at most 64 MiB of HBM per device.

v0:
```python
import math

import jax
import jax.numpy as jnp
from jax import lax
from jax.sharding import PartitionSpec as P

BLADES = 4
NEIGHBORS = 6
RIM = 16


def with_halo(cells, sides, width):
    for axis, dim in sides:
        count = lax.axis_size(axis)
        ends = count - 1
        head = lax.slice_in_dim(cells, 0, width, axis=dim)
        tail = lax.slice_in_dim(cells, cells.shape[dim] - width, cells.shape[dim], axis=dim)
        cells = jnp.concatenate(
            [
                lax.ppermute(tail, axis, [(i, (i + 1) % count) for i in range(ends)]),
                cells,
                lax.ppermute(head, axis, [((i + 1) % count, i) for i in range(ends)]),
            ],
            axis=dim,
        )
    return cells


def shifted(shard, axis, by):
    peers = lax.axis_size(axis)
    return lax.ppermute(shard, axis, [(i, (i + by) % peers) for i in range(peers)])


def flux_stack(values):
    density = values[0]
    safe_density = jnp.where(density > 0, density, 1.0)
    momenta = values[1:4]
    energy = values[4]
    speeds = momenta / safe_density
    pressure = 0.4 * (energy - 0.5 * jnp.sum(momenta * speeds, axis=0))
    result = []
    for direction in range(3):
        normal_speed = speeds[direction]
        pieces = [momenta[direction]]
        for component in range(3):
            product_term = momenta[component] * normal_speed
            if component == direction:
                product_term = product_term + pressure
            pieces.append(product_term)
        pieces.append((energy + pressure) * normal_speed)
        result.append(jnp.stack(pieces))
    return jnp.stack(result).astype(jnp.bfloat16)


def spectral_matrix(instances):
    positions = jnp.arange(instances, dtype=jnp.int32)
    offsets = positions[:, None] - positions[None, :]
    parity = 1.0 - 2.0 * (offsets % 2).astype(jnp.float32)
    angles = offsets.astype(jnp.float32) * (math.pi / instances)
    safe_angles = jnp.where(offsets == 0, 1.0, angles)
    return jnp.where(offsets == 0, 0.0, 0.5 * parity / jnp.tan(safe_angles))


def rotate_momenta(values, cosine, sine_turn):
    rotated_x = cosine * values[1] - sine_turn * values[2]
    rotated_y = sine_turn * values[1] + cosine * values[2]
    return jnp.stack([values[0], rotated_x, rotated_y, values[3], values[4]])


def body(
    flow_state,
    op_weight,
    adjacency,
    face_tile,
    face_row,
    face_partner,
    face_side,
    face_count,
    frequency,
):
    components, tiles_local, row_width = flow_state.shape
    tile_cells = op_weight.shape[1] // components
    inst_local = row_width // tile_cells
    dom_index = lax.axis_index("dom")
    inst_devices = lax.axis_size("inst")
    instances = inst_local * inst_devices
    lag_steps = instances // BLADES
    lag_devices = lag_steps // inst_local
    faces_local = face_partner.shape[0]
    weights = op_weight.reshape(NEIGHBORS + 3, components, tile_cells, components, tile_cells)
    padded_state = with_halo(flow_state, (("dom", 1),), RIM)
    padded_flux = flux_stack(padded_state)
    padded_flux = padded_flux.reshape(3, components, tiles_local + 2 * RIM, inst_local, tile_cells)
    local_adj = adjacency - (dom_index * tiles_local - RIM)
    accumulated = jnp.zeros((components, tiles_local, inst_local, tile_cells), jnp.float32)
    for neighbor in range(NEIGHBORS):
        picked = jnp.take(padded_flux[neighbor // 2], local_adj[:, neighbor], axis=1)
        accumulated = accumulated + jnp.einsum(
            "ctix,cxey->etiy", picked, weights[neighbor], preferred_element_type=jnp.float32
        )
    for direction in range(3):
        own_flux = padded_flux[direction][:, RIM : RIM + tiles_local]
        accumulated = accumulated + jnp.einsum(
            "ctix,cxey->etiy",
            own_flux,
            weights[NEIGHBORS + direction],
            preferred_element_type=jnp.float32,
        )
    wanted_tile, wanted_row = (
        lax.all_gather(face_partner, "dom", axis=0, tiled=True),
        lax.all_gather(face_row, "dom", axis=0, tiled=True),
    )
    owner_local = wanted_tile - dom_index * tiles_local
    owned_mask = ((owner_local >= 0) & (owner_local < tiles_local)).astype(jnp.float32)
    clipped = jnp.clip(owner_local, 0, tiles_local - 1)
    inst_offsets = jnp.arange(inst_local, dtype=jnp.int32) * tile_cells
    flat_state = flow_state.reshape(components, tiles_local * row_width)
    source_pos = clipped[:, None] * row_width + inst_offsets[None, :] + wanted_row[:, None]
    offered = flat_state[:, source_pos] * owned_mask[None, :, None]
    partner_vals = lax.psum_scatter(offered, "dom", scatter_dimension=1, tiled=True)
    spectral = spectral_matrix(instances)
    state_rows = flow_state.reshape(components * tiles_local, row_width)
    upper_vals = shifted(partner_vals, "inst", -lag_devices)
    lower_vals = shifted(partner_vals, "inst", lag_devices)
    moved_state = lax.all_to_all(state_rows, "inst", split_axis=0, concat_axis=1, tiled=True)
    row_count = moved_state.shape[0]
    shaped = moved_state.reshape(row_count, instances, tile_cells)
    applied = jnp.einsum("kj,rjx->rkx", spectral, shaped, precision=lax.Precision.HIGHEST)
    derivative = lax.all_to_all(
        applied.reshape(row_count, instances * tile_cells).astype(jnp.bfloat16),
        "inst",
        split_axis=1,
        concat_axis=0,
        tiled=True,
    ).astype(jnp.float32)
    accumulated = accumulated + frequency[0] * derivative.reshape(
        components, tiles_local, inst_local, tile_cells
    )
    flat_total = accumulated.reshape(components, tiles_local * row_width)
    live_mask = (jnp.arange(faces_local, dtype=jnp.int32) < face_count[0]).astype(jnp.float32)
    own_local = face_tile - dom_index * tiles_local
    own_pos = own_local[:, None] * row_width + inst_offsets[None, :] + face_row[:, None]
    own_vals = flat_state[:, own_pos]
    lagged = jnp.where((face_side == 1)[None, :, None], upper_vals, lower_vals)
    sine_turn = (jnp.where(face_side == 1, 1.0, -1.0) * math.sin(2.0 * math.pi / BLADES)).astype(
        jnp.float32
    )[:, None]
    cosine = math.cos(2.0 * math.pi / BLADES)
    rotated = rotate_momenta(lagged, cosine, sine_turn)
    change = live_mask[None, :, None] * (rotated - own_vals)
    flat_total = flat_total.at[:, own_pos].add(change)
    return flat_total.reshape(components, tiles_local, row_width)


def solution(mesh):
    placed = (
        P("groups", "dom", "inst"),
        P(),
        P("dom", None),
        P("dom"),
        P("dom"),
        P("dom"),
        P("dom"),
        P("dom"),
        P("groups"),
    )
    return jax.shard_map(
        body, mesh=mesh, in_specs=placed, out_specs=P("groups", "dom", "inst"), check_vma=False
    )
```

profile of v0, /device:TPU:0, one launch (start us, length us, event | category | flops | bytes accessed | tf_op | source)
XLA Modules:
  0.0 170.2 jit_solution(10390529501613284179)
XLA Ops:
  0.0 6.2 %all-gather = s32[4,1,256]{2,1,0:T(1,128)S(1)} all-gather(s32[1,1,256]{2,1,0:T(1,128)} %bitcast.198), channel_id=1, replica_groups=mesh['groups'=2,'inst'=4,'dom'=4] {'dom'}, dimensions={0}, use_global_device_ids=true | all-gather | bytes 5120 | tf_op jit(solution)/shard_map/all_gather | solution.py:111
  6.3 5.5 %all-gather.1 = s32[4,1,256]{2,1,0:T(1,128)S(1)} all-gather(s32[1,1,256]{2,1,0:T(1,128)} %bitcast.197), channel_id=1, replica_groups=mesh['groups'=2,'inst'=4,'dom'=4] {'dom'}, dimensions={0}, use_global_device_ids=true | all-gather | bytes 5120 | tf_op jit(solution)/shard_map/all_gather | solution.py:112
  12.4 5.9 %copy.168 = f32[5,128,128]{0,2,1:T(8,128)} copy(f32[5,128,128]{2,1,0:T(8,128)} %param.11) | data formatting | bytes 655360 | tf_op args[0]
  18.3 8.9 %gather_fusion = f32[2048,5]{1,0:T(8,128)S(1)} fusion(f32[5,16384]{0,1:T(8,128)} %bitcast.181, s32[2048]{0:T(1024)S(1)} %broadcast_clamp_fusion), kind=kCustom, calls=%fused_computation.6 | custom fusion | bytes 90112 | tf_op jit(solution)/shard_map/gather | solution.py:120
  27.2 2.9 %multiply_bitcast_fusion = f32[5,1024,2]{0,2,1:T(2,128)S(1)} fusion(f32[1024,2,5]{2,1,0:T(2,128)S(1)} %bitcast.185, f32[1024]{0:T(1024)S(1)} %bitcast.195), kind=kLoop, calls=%fused_computation.31 | loop fusion | flops 10240 | bytes 86016 | tf_op jit(solution)/shard_map/mul | solution.py:120
  30.2 26.5 %all-reduce = f32[5,1024,2]{0,2,1:T(2,128)S(1)} all-reduce(f32[5,1024,2]{0,2,1:T(2,128)S(1)} %multiply_bitcast_fusion), channel_id=2, replica_groups=mesh['groups'=2,'inst'=4,'dom'=4] {'dom'}, use_global_device_ids=true, to_apply=%region_1.3.clone | all-reduce | flops 10240 | bytes 81920
  56.7 0.6 dynamic-slice
  58.1 1.6 collective-permute-start.3
  59.7 2.2 %collective-permute-start.2 = (f32[5,256,2]{1,2,0:T(2,128)S(1)}, f32[5,256,2]{1,2,0:T(2,128)S(1)}, u32[]{:S(2)}, u32[]{:S(2)}) collective-permute-start(f32[5,256,2]{1,2,0:T(2,128)S(1)} %copy.169), channel_id=1, source_target_pairs={{0,12},{4,0},{8,4},{12,8},{1,13},{5,1},{9,5},{13,9},{2,14},{6,2},{... | collective-permute-start | bytes 30728 | tf_op jit(solution)/shard_map/ppermute | solution.py:32
  61.9 4.1 %all-to-all-start = ((f32[4,160,128]{2,1,0:T(8,128)}), f32[4,160,128]{2,1,0:T(8,128)}, u32[]{:S(2)}, u32[]{:S(2)}) async-start(f32[4,160,128]{2,1,0:T(8,128)} %bitcast.59), calls=%async_computation | async-start | bytes 655360 | tf_op jit(solution)/shard_map/all_to_all | solution.py:126
  66.1 0.8 fusion.89
  66.9 0.9 copy.136
  67.8 1.3 collective-permute-start.1
  69.1 0.9 copy.135
  70.0 3.8 %collective-permute-start = (f32[5,16,128]{1,2,0:T(8,128)}, f32[5,16,128]{1,2,0:T(8,128)}, u32[]{:S(2)}, u32[]{:S(2)}) collective-permute-start(f32[5,16,128]{1,2,0:T(8,128)} %copy.135), channel_id=1, source_target_pairs={{0,1},{1,2},{2,3},{4,5},{5,6},{6,7},{8,9},{9,10},{10,11},{12,13},{... | collective-permute-start | bytes 122888 | tf_op jit(solution)/shard_map/ppermute | solution.py:21
  74.5 0.6 compare_and_fusion.5
  75.1 0.6 pad_clamp_fusion.2
  76.0 2.6 %fusion.88 = (bf16[1,320,320]{2,1,0:T(8,128)(2,1)S(1)}, bf16[1,320,320]{2,1,0:T(8,128)(2,1)S(1)}, bf16[1,320,320]{2,1,0:T(8,128)(2,1)S(1)}, bf16[1,320,320]{2,1,...) fusion(bf16[9,320,320]{2,1,0:T(8,128)(2,1)} %param.12), kind=kLoop, calls=%fused_computation.173 | loop fusion | bytes 3686400 | tf_op jit(solution)/shard_map/slice | solution.py:100
  78.7 0.6 pad_clamp_fusion.1
  79.3 1.9 %copy.137 = f32[5,128,128]{1,2,0:T(8,128)} copy(f32[5,128,128]{2,1,0:T(8,128)} %param.11) | data formatting | bytes 655360 | tf_op args[0]
  82.0 1.2 copy.140
  83.4 0.4 copy.157
  84.1 1.1 copy.155
  85.5 1.1 copy.152
  86.9 0.4 copy.149
  87.5 0.4 copy.146
  88.2 0.4 copy.143
  88.6 1.2 squeeze.101
  89.8 0.4 copy.161
  90.5 0.4 copy.159
  90.9 4.4 %gather_fusion.1 = f32[512,5]{1,0:T(8,128)S(1)} fusion(f32[5,16384]{0,1:T(8,128)} %bitcast.182, s32[1024]{0:T(1024)S(1)} %pad_clamp_fusion), kind=kCustom, calls=%fused_computation.7 | custom fusion | bytes 22528 | tf_op jit(solution)/shard_map/gather | solution.py:144
  95.7 1.5 pad_maximum_fusion
  97.7 0.6 copy-done.2
  98.5 1.5 copy.150
  100.0 2.3 %gather_fusion.7 = bf16[128,5,2,64]{3,2,1,0:T(2,128)(2,1)} fusion(bf16[5,160,2,64]{3,2,1,0:T(2,128)(2,1)S(1)} %copy.150, s32[1024]{0:T(1024)} %get-tuple-element.64), kind=kCustom, calls=%fused_computation.5.clone | custom fusion | bytes 328192 | tf_op jit(solution)/shard_map/jit(_take)/gather | solution.py:98
  102.3 2.3 %gather_fusion.6 = bf16[128,5,2,64]{3,2,1,0:T(2,128)(2,1)} fusion(bf16[5,160,2,64]{3,2,1,0:T(2,128)(2,1)S(1)} %copy.150, s32[1024]{0:T(1024)} %pad_clamp_fusion.2), kind=kCustom, calls=%fused_computation.4.clone | custom fusion | bytes 328192 | tf_op jit(solution)/shard_map/jit(_take)/gather | solution.py:98
  104.6 1.5 copy.144
  106.1 2.2 %gather_fusion.5 = bf16[128,5,2,64]{3,2,1,0:T(2,128)(2,1)} fusion(bf16[5,160,2,64]{3,2,1,0:T(2,128)(2,1)S(1)} %copy.144, s32[1024]{0:T(1024)S(1)} %pad_clamp_fusion.3), kind=kCustom, calls=%fused_computation.3.clone | custom fusion | bytes 328192 | tf_op jit(solution)/shard_map/jit(_take)/gather | solution.py:98
  108.3 2.2 %gather_fusion.4 = bf16[128,5,2,64]{3,2,1,0:T(2,128)(2,1)} fusion(bf16[5,160,2,64]{3,2,1,0:T(2,128)(2,1)S(1)} %copy.144, s32[1024]{0:T(1024)S(1)} %pad_clamp_fusion.4), kind=kCustom, calls=%fused_computation.2.clone | custom fusion | bytes 328192 | tf_op jit(solution)/shard_map/jit(_take)/gather | solution.py:98
  110.5 1.5 copy.138
  112.0 2.0 %convolution_bitcast_fusion.2 = f32[128,2,5,64]{0,3,2,1:T(8,128)} fusion(bf16[5,64,5,64]{1,3,0,2:T(8,128)(2,1)S(1)} %copy.157, bf16[5,160,2,64]{1,3,2,0:T(8,128)(2,1)} %bitcast.189), kind=kOutput, calls=%fused_computation.13 | convolution fusion | flops 52428800 | bytes 696320 | tf_op jit(solution)/shard_map/ctix,cxey->etiy/dot_general | solution.py:104
  114.0 1.4 fusion.31
  115.4 2.2 %gather_fusion.3 = bf16[128,5,2,64]{3,2,1,0:T(2,128)(2,1)} fusion(bf16[5,160,2,64]{3,2,1,0:T(2,128)(2,1)S(1)} %copy.138, s32[1024]{0:T(1024)S(1)} %pad_clamp_fusion.5), kind=kCustom, calls=%fused_computation.1.clone | custom fusion | bytes 328192 | tf_op jit(solution)/shard_map/jit(_take)/gather | solution.py:98
  117.6 2.1 %convolution_bitcast_fusion.3 = f32[128,2,5,64]{0,3,2,1:T(8,128)} fusion(bf16[5,64,5,64]{1,3,0,2:T(8,128)(2,1)} %copy.155, bf16[5,128,2,64,1]{3,2,0,1,4:T(2,128)(2,1)S(1)} %fusion.31), kind=kOutput, calls=%fused_computation.14 | convolution fusion | flops 52428800 | bytes 696320 | tf_op jit(solution)/shard_map/ctix,cxey->etiy/dot_general | solution.py:99
  119.7 1.9 %fusion.29 = (bf16[5,128,2,64,1]{3,2,0,1,4:T(2,128)(2,1)S(1)}, bf16[5,128,2,64,1]{3,2,0,1,4:T(2,128)(2,1)S(1)}) fusion(bf16[128,5,2,64]{3,2,1,0:T(2,128)(2,1)} %gather_fusion.5, pred[128]{0:T(512)(128)(4,1)} %get-tuple-element.54, bf16[128,5,2,64]{3,2,1,0:T(2,128)(2,1)} %gather_fusion.6, pred[128]{0:T(512)(128)(4,1)} %get-tuple-element.52), kind=kLoop, calls=%fused_computation.62 | loop fusion | flops 163840 | bytes 655616 | tf_op jit(solution)/shard_map/jit(_take)/select_n | solution.py:98
  121.6 1.1 convolution_bitcast_fusion.4
  122.7 1.9 %fusion.27 = (bf16[5,128,2,64,1]{3,2,0,1,4:T(2,128)(2,1)S(1)}, bf16[5,128,2,64,1]{3,2,0,1,4:T(2,128)(2,1)S(1)}) fusion(bf16[128,5,2,64]{3,2,1,0:T(2,128)(2,1)} %gather_fusion.3, pred[128]{0:T(512)(128)(4,1)} %get-tuple-element.58, bf16[128,5,2,64]{3,2,1,0:T(2,128)(2,1)} %gather_fusion.4, pred[128]{0:T(512)(128)(4,1)} %get-tuple-element.56), kind=kLoop, calls=%fused_computation.60 | loop fusion | flops 163840 | bytes 655616 | tf_op jit(solution)/shard_map/jit(_take)/select_n | solution.py:98
  124.7 1.3 convolution_bitcast_fusion
  126.0 1.1 convolution_bitcast_fusion.5
  127.0 1.0 convolution_bitcast_fusion.6
  128.1 1.1 convolution_bitcast_fusion.7
  129.1 1.2 copy.162
  130.6 0.4 copy.163
  131.0 0.6 fusion
  132.1 0.7 copy.165
  132.8 5.0 %all-to-all-start.1 = ((bf16[160,4,128]{2,0,1:T(8,128)(2,1)}), bf16[160,4,128]{2,0,1:T(8,128)(2,1)S(1)}, u32[]{:S(2)}, u32[]{:S(2)}) async-start(bf16[160,4,128]{2,0,1:T(8,128)(2,1)} %copy.165), calls=%async_computation.1 | async-start | bytes 327680 | tf_op jit(solution)/shard_map/all_to_all | solution.py:130
  137.8 1.3 convolution_bitcast_fusion.1
  139.2 1.6 gather_fusion.2
  140.8 0.4 fusion.26
  141.2 3.3 %all-to-all-done.1 = bf16[160,4,128]{2,0,1:T(8,128)(2,1)S(1)} async-done(((bf16[160,4,128]{2,0,1:T(8,128)(2,1)}), bf16[160,4,128]{2,0,1:T(8,128)(2,1)S(1)}, u32[]{:S(2)}, u32[]{:S(2)}) %all-to-all-start.1) | async-done | bytes 163872 | tf_op jit(solution)/shard_map/all_to_all | solution.py:130
  145.1 1.9 %fusion.10 = f32[5,128,2,64]{1,3,0,2:T(8,128)S(1)} fusion(f32[5,128,2,64]{1,3,0,2:T(8,128)S(1)} %copy.166, f32[128,2,5,64]{0,3,2,1:T(8,128)S(1)} %convolution_bitcast_fusion, f32[128,2,5,64]{0,3,2,1:T(8,128)S(1)} %convolution_bitcast_fusion.1, f32[128,2,5,64]{0,3,2,1:T(8,128)} %convolution_bitcast_fusion.2, ...), kind=kOutput, calls=%fused_computation.30 | convolution fusion | flops 53166080 | bytes 3645440 | tf_op jit(solution)/shard_map/ctix,cxey->etiy/dot_general | solution.py:99
  147.0 7.7 %copy.205 = f32[5,128,2,64]{0,3,2,1:T(8,128)} copy(f32[5,128,2,64]{1,3,0,2:T(8,128)S(1)} %fusion.10) | data formatting | bytes 655360 | tf_op jit(solution)/shard_map/reshape | solution.py:140
  154.7 9.6 %scatter_fusion = f32[5,16384]{0,1:T(8,128)} fusion(f32[5,16384]{0,1:T(8,128)} %bitcast.183, s32[512]{0:T(512)S(1)} %reshape.326, f32[512,5]{1,0:T(8,128)S(1)} %bitcast.186), kind=kCustom, calls=%fused_computation.8 | custom fusion | flops 2560 | bytes 32768 | tf_op jit(solution)/shard_map/scatter-add | solution.py:152
  164.3 5.9 %copy.174 = f32[5,128,128]{2,1,0:T(8,128)} copy(f32[5,128,128]{0,2,1:T(8,128)} %bitcast.184) | data formatting | bytes 655360 | tf_op jit(solution)/shard_map/reshape | solution.py:153
  (73 shorter events, 5.4 us)
Async XLA Ops:
  18.3 38.4 %copy-start.10 = (u32[32]{0:T(128)S(1)}, u32[32]{0:T(128)}, u32[]{:S(2)}) copy-start(u32[32]{0:T(128)} %constant.42) | copy-start | bytes 388
  18.3 56.1 %copy-start.8 = (s32[256]{0:T(256)S(1)}, s32[256]{0:T(256)}, u32[]{:S(2)}) copy-start(s32[256]{0:T(256)} %param.14) | copy-start | bytes 3076
  18.3 56.1 %copy-start.9 = (s32[256]{0:T(256)S(1)}, s32[256]{0:T(256)}, u32[]{:S(2)}) copy-start(s32[256]{0:T(256)} %param.17) | copy-start | bytes 3076
  18.3 56.1 %copy-start.6 = (s32[128,6]{0,1:T(8,128)S(1)}, s32[128,6]{0,1:T(8,128)}, u32[]{:S(2)}) copy-start(s32[128,6]{0,1:T(8,128)} %param.13) | copy-start | bytes 9220
  18.3 57.4 %copy-start.5 = (s32[256]{0:T(256)S(1)}, s32[256]{0:T(256)}, u32[]{:S(2)}) copy-start(s32[256]{0:T(256)} %param.15) | copy-start | bytes 3076
  58.1 37.3 %collective-permute-start.3 = (f32[5,256,2]{1,2,0:T(2,128)S(1)}, f32[5,256,2]{1,2,0:T(2,128)S(1)}, u32[]{:S(2)}, u32[]{:S(2)}) collective-permute-start(f32[5,256,2]{1,2,0:T(2,128)S(1)} %copy.169), channel_id=1, source_target_pairs={{0,4},{4,8},{8,12},{12,0},{1,5},{5,9},{9,13},{13,1},{2,6},{6,10},{... | collective-permute-start | bytes 30728 | tf_op jit(solution)/shard_map/ppermute | solution.py:32
  59.7 35.7 %collective-permute-start.2 = (f32[5,256,2]{1,2,0:T(2,128)S(1)}, f32[5,256,2]{1,2,0:T(2,128)S(1)}, u32[]{:S(2)}, u32[]{:S(2)}) collective-permute-start(f32[5,256,2]{1,2,0:T(2,128)S(1)} %copy.169), channel_id=1, source_target_pairs={{0,12},{4,0},{8,4},{12,8},{1,13},{5,1},{9,5},{13,9},{2,14},{6,2},{... | collective-permute-start | bytes 30728 | tf_op jit(solution)/shard_map/ppermute | solution.py:32
  61.9 67.2 %all-to-all-start = ((f32[4,160,128]{2,1,0:T(8,128)}), f32[4,160,128]{2,1,0:T(8,128)}, u32[]{:S(2)}, u32[]{:S(2)}) async-start(f32[4,160,128]{2,1,0:T(8,128)} %bitcast.59), calls=%async_computation | async-start | bytes 655360 | tf_op jit(solution)/shard_map/all_to_all | solution.py:126
  67.8 27.9 %collective-permute-start.1 = (f32[5,16,128]{1,2,0:T(8,128)}, f32[5,16,128]{1,2,0:T(8,128)}, u32[]{:S(2)}, u32[]{:S(2)}) collective-permute-start(f32[5,16,128]{1,2,0:T(8,128)} %copy.136), channel_id=1, source_target_pairs={{1,0},{2,1},{3,2},{5,4},{6,5},{7,6},{9,8},{10,9},{11,10},{13,12},{... | collective-permute-start | bytes 122888 | tf_op jit(solution)/shard_map/ppermute | solution.py:23
  70.0 25.7 %collective-permute-start = (f32[5,16,128]{1,2,0:T(8,128)}, f32[5,16,128]{1,2,0:T(8,128)}, u32[]{:S(2)}, u32[]{:S(2)}) collective-permute-start(f32[5,16,128]{1,2,0:T(8,128)} %copy.135), channel_id=1, source_target_pairs={{0,1},{1,2},{2,3},{4,5},{5,6},{6,7},{8,9},{9,10},{10,11},{12,13},{... | collective-permute-start | bytes 122888 | tf_op jit(solution)/shard_map/ppermute | solution.py:21
  95.7 25.9 %copy-start = (bf16[5,64,5,64]{1,3,0,2:T(8,128)(2,1)S(1)}, bf16[5,64,5,64]{1,3,0,2:T(8,128)(2,1)}, u32[]{:S(2)}) copy-start(bf16[5,64,5,64]{1,3,0,2:T(8,128)(2,1)} %copy.152) | copy-start | bytes 614404
  97.6 0.7 copy-start.2
  97.7 0.8 copy-start.3
  97.7 0.9 copy-start.4
  114.0 26.7 %copy-start.7 = (pred[128]{0:T(512)(128)(4,1)S(1)}, pred[128]{0:T(512)(128)(4,1)}, u32[]{:S(2)}) copy-start(pred[128]{0:T(512)(128)(4,1)} %get-tuple-element.8) | copy-start | bytes 388
  121.6 23.5 %copy-start.1 = (bf16[5,64,5,64]{1,3,0,2:T(8,128)(2,1)S(1)}, bf16[5,64,5,64]{1,3,0,2:T(8,128)(2,1)}, u32[]{:S(2)}) copy-start(bf16[5,64,5,64]{1,3,0,2:T(8,128)(2,1)} %copy.140) | copy-start | bytes 614404
  132.8 11.6 %all-to-all-start.1 = ((bf16[160,4,128]{2,0,1:T(8,128)(2,1)}), bf16[160,4,128]{2,0,1:T(8,128)(2,1)S(1)}, u32[]{:S(2)}, u32[]{:S(2)}) async-start(bf16[160,4,128]{2,0,1:T(8,128)(2,1)} %copy.165), calls=%async_computation.1 | async-start | bytes 327680 | tf_op jit(solution)/shard_map/all_to_all | solution.py:130
where the time goes:
time: 171 us; the launch traced here: 170 us
  local copies, waits for them, and re-layouts  72.2 us (42%)
  blocking collectives  38.2 us (22%)
  other arithmetic  22.5 us (13%)
  starting transfers between devices  18 us (11%)
  matrix products  13.5 us (8%)
  waiting for transfers between devices  3.27 us (2%)
  between operations  2.55 us (1%)
    unnamed x1, blocking collectives  26.5 us
    gather x6, local copies, waits for them, and re-layouts, body(): jnp.take(padded_flux[neighbor // 2], local_adj[:, neighbor], axis=1)  12.9 us
    scatter-add x1, other arithmetic, body(): flat_total = flat_total.at[:, own_pos].add(change)  9.61 us
    unnamed x27, local copies, waits for them, and re-layouts  9.28 us
    gather x1, local copies, waits for them, and re-layouts, body(): offered = flat_state[:, source_pos] * owned_mask[None, :, None]  8.89 us
    dot_general x6, matrix products, body(): jnp.einsum('ctix,cxey->etiy', picked, weights[neighbor], preferred_elemen...  8.18 us
    reshape x1, local copies, waits for them, and re-layouts, body(): flat_total = accumulated.reshape(components, tiles_local * row_width)  7.66 us
    all_gather x1, blocking collectives, body(): lax.all_gather(face_partner, 'dom', axis=0, tiled=True)  6.24 us
  transfers between devices with their start and end apart: 6, of which 1 were waited for; matrix products, arithmetic and copies ran while one was open for 35% of the time, Pallas kernels for 0%

commit v1 on v0

v1 whole, which is shorter than its diff:
```python
import functools
import math

import jax
import jax.numpy as jnp
from jax import lax
from jax.experimental import pallas as pl
from jax.experimental.pallas import tpu as pltpu
from jax.sharding import PartitionSpec as P

BLADES = 4
NEIGHBORS = 6
RIM = 16
MESH = pl.DeviceIdType.MESH
CHUNK = 16


def derivative_entry(offset, instances):
    offset %= instances
    if offset == 0 or 2 * offset == instances:
        return 0.0
    return 0.5 * (-1.0) ** offset / math.tan(math.pi * offset / instances)


def fluxes(values):
    density = values[0]
    safe_density = jnp.where(density > 0, density, 1.0)
    momenta = values[1:4]
    energy = values[4]
    speeds = [m / safe_density for m in momenta]
    kinetic = momenta[0] * speeds[0] + momenta[1] * speeds[1] + momenta[2] * speeds[2]
    pressure = 0.4 * (energy - 0.5 * kinetic)
    result = []
    for direction in range(3):
        pieces = [momenta[direction]]
        for component in range(3):
            term = momenta[component] * speeds[direction]
            pieces.append(term + pressure if component == direction else term)
        pieces.append((energy + pressure) * speeds[direction])
        result.append(pieces)
    return result


def kernel(
    peers_inst, peers_dom, cells,
    flow, weight, adj, face_tile, face_row, face_partner, face_side, count, freq,
    out,
    ubf, ain, tout, tin, stage, halo, wv, fp, ut, codes, pout, pin, acc,
    w_sem, code_sem, halo_sem, a_sem, t_sem, p_sem,
):
    n, ndom = peers_inst, peers_dom
    comps, tiles, width = flow.shape
    faces = face_tile.shape[1]
    slots = width // cells
    instances = n * slots
    lag = instances // BLADES // slots
    part = tiles // n
    ops = weight.shape[0]
    per_op = comps * cells
    aligned = part % CHUNK == 0
    rows = ubf.shape[1]
    wide = fp.shape[2] // slots
    shift = cells.bit_length() - 1
    me_i = lax.axis_index("inst")
    me_d = lax.axis_index("dom")

    def inst_at(step):
        return lax.rem(me_i + (step % n), n)

    def dom_at(step):
        return lax.rem(me_d + (step % ndom), ndom)

    def at(dom_step, inst_step):
        return {"inst": inst_at(inst_step), "dom": dom_at(dom_step)}

    def remote(src, dst, sems, index, target):
        return pltpu.make_async_remote_copy(
            src_ref=src,
            dst_ref=dst,
            send_sem=sems.at[(0,) + index],
            recv_sem=sems.at[(1,) + index],
            device_id=target,
            device_id_type=MESH,
        )

    partners = {(j, 0) for j in range(1, ndom)} | {(0, i) for i in range(1, n)}
    partners |= {(j, s % n) for j in range(ndom) for s in (lag, -lag)}
    partners = sorted(partners)
    barrier = pltpu.get_barrier_semaphore()
    for dom_step, inst_step in partners:
        pl.semaphore_signal(
            barrier, inc=1, device_id=at(dom_step, inst_step), device_id_type=MESH
        )
    weights_in = pltpu.make_async_copy(weight, wv, w_sem)
    weights_in.start()

    code = face_partner[...] * cells + face_row[...]
    codes[0] = jnp.broadcast_to(code, (8, faces))
    for p in range(n):
        if aligned:
            for c in range(comps):
                ubf[p, c * part : (c + 1) * part] = flow[
                    c, p * part : (p + 1) * part
                ].astype(jnp.bfloat16)
        else:
            stage[...] = jnp.zeros_like(stage)
            for c in range(comps):
                stage[c * part : (c + 1) * part] = flow[c, p * part : (p + 1) * part]
            ubf[p] = stage[...].astype(jnp.bfloat16)
    pl.semaphore_wait(barrier, len(partners))

    code_copies = [
        remote(codes.at[0], codes.at[j], code_sem, (j,), at(j, 0)) for j in range(1, ndom)
    ]
    for copy in code_copies:
        copy.start()
    a_copies = [
        remote(ubf.at[inst_at(i)], ain.at[i], a_sem, (i,), at(0, i)) for i in range(1, n)
    ]
    for copy in a_copies:
        copy.start()
    halo_copies = [
        remote(flow.at[:, tiles - RIM :], halo.at[0], halo_sem, (0,), at(1, 0)),
        remote(flow.at[:, :RIM], halo.at[1], halo_sem, (1,), at(-1, 0)),
    ]
    for copy in halo_copies:
        copy.start()

    low_lanes = lax.broadcasted_iota(jnp.int32, (CHUNK, width), 1) < cells

    def swap(value):
        return pltpu.roll(value, cells, 1)

    def put_fluxes(read, base):
        for direction, pieces in enumerate(fluxes(read)):
            for pair in range((comps + 1) // 2):
                first = pieces[2 * pair]
                cols = slice(pair * width, (pair + 1) * width)
                more = slice(wide + pair * width, wide + (pair + 1) * width)
                if 2 * pair + 1 < comps:
                    second = pieces[2 * pair + 1]
                    left = jnp.where(low_lanes, first, swap(second))
                    right = jnp.where(low_lanes, swap(first), second)
                else:
                    left, right = first, swap(first)
                fp[direction, base : base + CHUNK, cols] = left.astype(jnp.bfloat16)
                fp[direction, base : base + CHUNK, more] = right.astype(jnp.bfloat16)

    for c in range(comps):
        ut[c * width : (c + 1) * width] = flow[c].T.astype(jnp.bfloat16)
    for t in range(0, tiles, CHUNK):
        put_fluxes([flow[c, t : t + CHUNK] for c in range(comps)], RIM + t)

    cell_ids = lax.broadcasted_iota(jnp.int32, (cells, faces), 0)
    tile_ids = lax.broadcasted_iota(jnp.int32, (tiles, faces), 0)
    p_copies = []
    for j in range(ndom):
        if j:
            code_copies[j - 1].wait_recv()
        wanted = codes[j][:1]
        wanted_tile = lax.shift_right_logical(wanted, shift) - me_d * tiles
        wanted_cell = lax.bitwise_and(wanted, cells - 1)
        pick = jnp.where(tile_ids == wanted_tile, 1.0, 0.0).astype(jnp.bfloat16)
        found = jnp.dot(ut[...], pick, preferred_element_type=jnp.float32)
        mask = cell_ids == wanted_cell
        lines = [
            jnp.sum(
                jnp.where(mask, found[g * cells : (g + 1) * cells], 0.0),
                axis=0,
                keepdims=True,
            )
            for g in range(comps * slots)
        ]
        lines.append(jnp.zeros((pout.shape[1] - comps * slots, faces), jnp.float32))
        pout[j] = jnp.concatenate(lines, axis=0).astype(jnp.bfloat16)
        for way, step in enumerate((-lag, lag)):
            copy = remote(pout.at[j], pin.at[way, j], p_sem, (way, j), at(-j, step))
            copy.start()
            p_copies.append(copy)

    for copy in a_copies:
        copy.wait_recv()
    cross = [
        jnp.where(
            low_lanes,
            derivative_entry(2 * delta - 1, instances),
            derivative_entry(2 * delta + 1, instances),
        ).astype(jnp.float32)
        for delta in range(n)
    ]
    for r in range(0, rows, CHUNK):
        plain = [
            (ubf[me_i, r : r + CHUNK] if i == 0 else ain[i, r : r + CHUNK]).astype(jnp.float32)
            for i in range(n)
        ]
        turned = [swap(value) for value in plain]
        for m in range(n):
            total = jnp.zeros((CHUNK, width), jnp.float32)
            for i in range(n):
                even = derivative_entry(2 * (m + i), instances)
                if even != 0.0:
                    total = total + even * plain[i]
                total = total + cross[(m + i) % n] * turned[i]
            total = total.astype(jnp.bfloat16)
            if m == 0:
                tin[me_i, r : r + CHUNK] = total
            else:
                tout[m, r : r + CHUNK] = total
    t_copies = [
        remote(tout.at[m], tin.at[me_i], t_sem, (m,), at(0, m)) for m in range(1, n)
    ]
    for copy in t_copies:
        copy.start()

    weights_in.wait()

    def apply(left, right, op):
        w = wv[op]
        both = jnp.concatenate([left, right], axis=0)
        return jnp.dot(both, w, preferred_element_type=jnp.float32)

    total = None
    for direction in range(3):
        own = fp[direction, RIM : RIM + tiles]
        term = apply(own[:, :per_op], own[:, wide : wide + per_op], NEIGHBORS + direction)
        total = term if total is None else total + term

    for copy in halo_copies:
        copy.wait_recv()
    for side, base in ((0, 0), (1, RIM + tiles)):
        put_fluxes([halo[side, c] for c in range(comps)], base)
    neighbor_ids = lax.broadcasted_iota(jnp.int32, (tiles, tiles + 2 * RIM), 1)
    shifted = adj[...] - (me_d * tiles - RIM)
    for direction in range(3):
        pick = jnp.concatenate(
            [
                jnp.where(shifted[:, s : s + 1] == neighbor_ids, 1.0, 0.0).astype(jnp.bfloat16)
                for s in (2 * direction, 2 * direction + 1)
            ],
            axis=0,
        )
        picked = jnp.dot(pick, fp[direction], preferred_element_type=jnp.float32)
        picked = picked.astype(jnp.bfloat16)
        for s in range(2):
            block = picked[s * tiles : (s + 1) * tiles]
            total = total + apply(
                block[:, :per_op], block[:, wide : wide + per_op], 2 * direction + s
            )
    acc[:, :per_op] = total

    side = face_side[...] == 1
    live = lax.broadcasted_iota(jnp.int32, (1, faces), 1) < count[0]
    own_tile = jnp.where(live, face_tile[...] - me_d * tiles, -1)
    place = jnp.where(tile_ids == own_tile, 1.0, 0.0).astype(jnp.bfloat16)
    mask = cell_ids == face_row[...]
    ones = jnp.where(mask, 1.0, 0.0).astype(jnp.bfloat16)
    contract = (((1,), (1,)), ((), ()))
    times = lax.dot_general(
        place, jnp.concatenate([ones] * slots, axis=0), contract,
        preferred_element_type=jnp.float32,
    )
    for copy in p_copies:
        copy.wait_recv()
    upper = pin[0, 0].astype(jnp.float32)
    lower = pin[1, 0].astype(jnp.float32)
    for j in range(1, ndom):
        upper = upper + pin[0, j].astype(jnp.float32)
        lower = lower + pin[1, j].astype(jnp.float32)
    lagged = jnp.where(side, upper, lower)
    lines = [lagged[g : g + 1] for g in range(comps * slots)]
    cosine = math.cos(2.0 * math.pi / BLADES)
    sine = jnp.where(side, 1.0, -1.0) * math.sin(2.0 * math.pi / BLADES)
    for k in range(slots):
        m0, m1 = lines[slots + k], lines[2 * slots + k]
        lines[slots + k] = cosine * m0 - sine * m1
        lines[2 * slots + k] = sine * m0 + cosine * m1
    spread = jnp.concatenate(
        [jnp.where(mask, line, 0.0).astype(jnp.bfloat16) for line in lines], axis=0
    )
    gained = lax.dot_general(place, spread, contract, preferred_element_type=jnp.float32)

    for copy in t_copies:
        copy.wait_recv()
    speed = freq[0]
    low = lax.broadcasted_iota(jnp.int32, (part, width), 1) < cells
    for p in range(n):
        span = slice(p * part, (p + 1) * part)
        more = slice(tiles + p * part, tiles + (p + 1) * part)
        if not aligned:
            stage[...] = tin[p].astype(jnp.float32)
        for c in range(comps):
            pair = c // 2
            cols = slice(pair * width, (pair + 1) * width)
            if c % 2 == 0:
                spatial = jnp.where(low, acc[span, cols], swap(acc[more, cols]))
            else:
                spatial = jnp.where(low, swap(acc[span, cols]), acc[more, cols])
            block = slice(c * part, (c + 1) * part)
            temporal = tin[p, block].astype(jnp.float32) if aligned else stage[block]
            out[c, span] = (
                spatial
                + speed * temporal
                + gained[span, c * width : (c + 1) * width]
                - times[span] * flow[c, span]
            )

    for copy in code_copies + a_copies + halo_copies + p_copies + t_copies:
        copy.wait_send()


def body(
    n, ndom,
    flow_state, op_weight, adjacency, face_tile, face_row, face_partner, face_side,
    face_count, frequency,
):
    comps, tiles, width = flow_state.shape
    ops, per_op, _ = op_weight.shape
    cells = per_op // comps
    faces = face_tile.shape[0]
    slots = width // cells
    rows = -(-(comps * (tiles // n)) // CHUNK) * CHUNK
    wide = -(-comps // 2) * width
    packed = -(-(comps * slots) // 16) * 16
    in_vmem = pl.BlockSpec(memory_space=pltpu.VMEM)
    in_smem = pl.BlockSpec(memory_space=pltpu.SMEM)
    bf16, f32 = jnp.bfloat16, jnp.float32
    dma = pltpu.SemaphoreType.DMA
    line = lambda values: values.reshape(1, faces)
    return pl.pallas_call(
        functools.partial(kernel, n, ndom, cells),
        out_shape=jax.ShapeDtypeStruct(flow_state.shape, f32),
        in_specs=[in_vmem, pl.BlockSpec(memory_space=pl.ANY)] + [in_vmem] * 5 + [in_smem] * 2,
        out_specs=in_vmem,
        scratch_shapes=[
            pltpu.VMEM((n, rows, width), bf16),
            pltpu.VMEM((n, rows, width), bf16),
            pltpu.VMEM((n, rows, width), bf16),
            pltpu.VMEM((n, rows, width), bf16),
            pltpu.VMEM((rows, width), f32),
            pltpu.VMEM((2, comps, RIM, width), f32),
            pltpu.VMEM(op_weight.shape, bf16),
            pltpu.VMEM((3, tiles + 2 * RIM, slots * wide), bf16),
            pltpu.VMEM((comps * width, tiles), bf16),
            pltpu.VMEM((ndom, 8, faces), jnp.int32),
            pltpu.VMEM((ndom, packed, faces), bf16),
            pltpu.VMEM((2, ndom, packed, faces), bf16),
            pltpu.VMEM((slots * tiles, wide), f32),
            dma,
            dma((2, ndom)),
            dma((2, 2)),
            dma((2, n)),
            dma((2, n)),
            dma((2, 2, ndom)),
        ],
        compiler_params=pltpu.CompilerParams(
            collective_id=0, has_side_effects=True, vmem_limit_bytes=40 * 1024 * 1024
        ),
    )(
        flow_state, op_weight, adjacency, line(face_tile), line(face_row),
        line(face_partner), line(face_side), face_count, frequency,
    )


def solution(mesh):
    placed = (
        P("groups", "dom", "inst"),
        P(),
        P("dom", None),
        P("dom"),
        P("dom"),
        P("dom"),
        P("dom"),
        P("dom"),
        P("groups"),
    )
    return jax.shard_map(
        functools.partial(body, mesh.shape["inst"], mesh.shape["dom"]),
        mesh=mesh,
        in_specs=placed,
        out_specs=P("groups", "dom", "inst"),
        check_vma=False,
    )
```

time: 171 us -> 25.2 us (0.15)
  local copies, waits for them, and re-layouts: 72.2 us -> 6.83 us
  blocking collectives: 38.2 us -> 0 us
  other arithmetic: 22.5 us -> 0 us
  starting transfers between devices: 18 us -> 0 us
  Pallas kernels: 0 us -> 16.7 us
  matrix products: 13.5 us -> 0 us
  waiting for transfers between devices: 3.27 us -> 0 us
    unnamed x1 -> x0, blocking collectives: 26.5 us -> none
    gather x9 -> x0, local copies, waits for them, and re-layouts: 26.3 us -> none  [the longest x6 12.9 us: body(): jnp.take(padded_flux[neighbor // 2], local_adj[:, neighbor], axis=1)]
    pallas_call x0 -> x1, Pallas kernels: none -> 16.7 us  [body(): pl.pallas_call(functools.partial(kernel, n, ndom, cells), out_shape=jax.S...]
    reshape x4 -> x0, local copies, waits for them, and re-layouts: 14.2 us -> none  [the longest x1 7.66 us: body(): flat_total = accumulated.reshape(components, tiles_local * row_width)]
    dot_general x10 -> x0, matrix products: 13.5 us -> none  [the longest x6 8.18 us: body(): jnp.einsum('ctix,cxey->etiy', picked, weights[neighbor], preferred_elemen...]
    squeeze x21 -> x0, local copies, waits for them, and re-layouts: 13.4 us -> none  [the longest x12 6.12 us: body(): weights[neighbor]]
    all_gather x2 -> x0, blocking collectives: 11.8 us -> none  [the longest x1 6.24 us: body(): lax.all_gather(face_partner, 'dom', axis=0, tiled=True)]
    scatter-add x1 -> x0, other arithmetic: 9.61 us -> none  [body(): flat_total = flat_total.at[:, own_pos].add(change)]
  transfers between devices with their start and end apart: 6 -> 0, of which waited for: 1 -> 0; matrix products, arithmetic and copies ran while one was open for 35% -> 0% of each run, Pallas kernels for 0% -> 0%
where the time goes in v1:
time: 25.2 us; the launch traced here: 24.9 us
  Pallas kernels  16.7 us (66%)
  local copies, waits for them, and re-layouts  6.83 us (27%)
  between operations  1.32 us (5%)
    pallas_call x1, Pallas kernels, body(): pl.pallas_call(functools.partial(kernel, n, ndom, cells), out_shape=jax.S...  16.7 us
    unnamed x14, local copies, waits for them, and re-layouts  6.83 us

profile of v1, /device:TPU:0, one launch (start us, length us, event | category | flops | bytes accessed | tf_op | source)
XLA Modules:
  0.0 24.9 jit_solution(1538106841709777646)
XLA Ops:
  1.3 0.8 %copy.10.adj = s32[128,6]{1,0:T(8,128)S(1)} copy(s32[128,6]{0,1:T(8,128)} %param.11) | data formatting | bytes 6144 | tf_op args[2]
  2.1 0.0 copy-start
  2.1 1.6 %copy-done = bf16[9,320,320]{2,1,0:T(8,128)(2,1)S(1)} copy-done((bf16[9,320,320]{2,1,0:T(8,128)(2,1)S(1)}, bf16[9,320,320]{2,1,0:T(8,128)(2,1)}, u32[]{:S(2)}) %copy-start) | copy-done | bytes 1843224
  3.7 0.0 copy-start.1
  3.7 1.0 %copy-done.1 = f32[5,128,128]{2,1,0:T(8,128)S(1)} copy-done((f32[5,128,128]{2,1,0:T(8,128)S(1)}, f32[5,128,128]{2,1,0:T(8,128)}, u32[]{:S(2)}) %copy-start.1) | copy-done | bytes 327704
  4.7 0.0 copy-start.2
  4.7 0.7 %copy-done.2 = s32[256]{0:T(256)S(1)} copy-done((s32[256]{0:T(256)S(1)}, s32[256]{0:T(256)}, u32[]{:S(2)}) %copy-start.2) | copy-done | bytes 1048
  5.4 0.0 copy-start.3
  5.4 0.7 %copy-done.3 = s32[256]{0:T(256)S(1)} copy-done((s32[256]{0:T(256)S(1)}, s32[256]{0:T(256)}, u32[]{:S(2)}) %copy-start.3) | copy-done | bytes 1048
  6.0 0.0 copy-start.4
  6.0 0.7 %copy-done.4 = s32[256]{0:T(256)S(1)} copy-done((s32[256]{0:T(256)S(1)}, s32[256]{0:T(256)}, u32[]{:S(2)}) %copy-start.4) | copy-done | bytes 1048
  6.7 0.0 copy-start.5
  6.7 0.7 %copy-done.5 = s32[256]{0:T(256)S(1)} copy-done((s32[256]{0:T(256)S(1)}, s32[256]{0:T(256)}, u32[]{:S(2)}) %copy-start.5) | copy-done | bytes 1048
  7.4 16.7 %shard_map.91 = f32[5,128,128]{2,1,0:T(8,128)S(1)} custom-call(f32[5,128,128]{2,1,0:T(8,128)S(1)} %copy-done.1, bf16[9,320,320]{2,1,0:T(8,128)(2,1)S(1)} %copy-done, s32[128,6]{1,0:T(8,128)S(1)} %copy.10.adj, s32[1,256]{1,0:T(1,128)S(1)} %bitcast.4, s32[1,256]{1,0:T(1,128)S(1)} %bitcast.5, s32[1,256]{1,0:T(1,128)S(1)} %bitcast.6, s32[1,256]{1,0:T(1,128)S(1)} %bitcast.7, ...), custom_call_target="tpu_custom_call" | custom-call | tf_op jit(solution)/shard_map/pallas_call | solution.py:329
  24.2 0.7 %copy.14 = f32[5,128,128]{2,1,0:T(8,128)} copy(f32[5,128,128]{2,1,0:T(8,128)S(1)} %shard_map.91) | data formatting | bytes 655360
Async XLA Ops:
  2.1 1.6 %copy-start = (bf16[9,320,320]{2,1,0:T(8,128)(2,1)S(1)}, bf16[9,320,320]{2,1,0:T(8,128)(2,1)}, u32[]{:S(2)}) copy-start(bf16[9,320,320]{2,1,0:T(8,128)(2,1)} %weight.1) | copy-start | bytes 5529604
  3.7 1.0 %copy-start.1 = (f32[5,128,128]{2,1,0:T(8,128)S(1)}, f32[5,128,128]{2,1,0:T(8,128)}, u32[]{:S(2)}) copy-start(f32[5,128,128]{2,1,0:T(8,128)} %flow.1) | copy-start | bytes 983044
  4.7 0.7 %copy-start.2 = (s32[256]{0:T(256)S(1)}, s32[256]{0:T(256)}, u32[]{:S(2)}) copy-start(s32[256]{0:T(256)} %param.12) | copy-start | bytes 3076
  5.4 0.7 %copy-start.3 = (s32[256]{0:T(256)S(1)}, s32[256]{0:T(256)}, u32[]{:S(2)}) copy-start(s32[256]{0:T(256)} %param.13) | copy-start | bytes 3076
  6.0 0.7 %copy-start.4 = (s32[256]{0:T(256)S(1)}, s32[256]{0:T(256)}, u32[]{:S(2)}) copy-start(s32[256]{0:T(256)} %param.14) | copy-start | bytes 3076
  6.7 0.7 %copy-start.5 = (s32[256]{0:T(256)S(1)}, s32[256]{0:T(256)}, u32[]{:S(2)}) copy-start(s32[256]{0:T(256)} %param.15) | copy-start | bytes 3076

commit v2 on v1

--- a/solution.py
+++ b/solution.py
@@ -43,10 +43,11 @@
 
 def kernel(
     peers_inst, peers_dom, cells,
-    flow, weight, adj, face_tile, face_row, face_partner, face_side, count, freq,
+    flow_in, weight, adj_in, tile_in, row_in, partner_in, side_in, count_in, freq_in,
     out,
+    flow, adj, face_tile, face_row, face_partner, face_side, count, freq,
     ubf, ain, tout, tin, stage, halo, wv, fp, ut, codes, pout, pin, acc,
-    w_sem, code_sem, halo_sem, a_sem, t_sem, p_sem,
+    in_sem, code_sem, halo_sem, a_sem, t_sem, p_sem,
 ):
     n, ndom = peers_inst, peers_dom
     comps, tiles, width = flow.shape
@@ -91,11 +92,31 @@
         pl.semaphore_signal(
             barrier, inc=1, device_id=at(dom_step, inst_step), device_id_type=MESH
         )
-    weights_in = pltpu.make_async_copy(weight, wv, w_sem)
-    weights_in.start()
-
+    arriving = [
+        pltpu.make_async_copy(src, dst, in_sem.at[i])
+        for i, (src, dst) in enumerate(
+            (
+                (flow_in, flow),
+                (partner_in, face_partner),
+                (row_in, face_row),
+                (adj_in, adj),
+                (tile_in, face_tile),
+                (side_in, face_side),
+                (count_in, count),
+                (freq_in, freq),
+                (weight, wv),
+            )
+        )
+    ]
+    for copy in arriving:
+        copy.start()
+    flow_copy, partner_copy, row_copy, *other_copies, weight_copy = arriving
+
+    partner_copy.wait()
+    row_copy.wait()
     code = face_partner[...] * cells + face_row[...]
     codes[0] = jnp.broadcast_to(code, (8, faces))
+    flow_copy.wait()
     for p in range(n):
         if aligned:
             for c in range(comps):
@@ -120,8 +141,8 @@
     for copy in a_copies:
         copy.start()
     halo_copies = [
-        remote(flow.at[:, tiles - RIM :], halo.at[0], halo_sem, (0,), at(1, 0)),
-        remote(flow.at[:, :RIM], halo.at[1], halo_sem, (1,), at(-1, 0)),
+        remote(flow_in.at[:, tiles - RIM :], halo.at[0], halo_sem, (0,), at(1, 0)),
+        remote(flow_in.at[:, :RIM], halo.at[1], halo_sem, (1,), at(-1, 0)),
     ]
     for copy in halo_copies:
         copy.start()
@@ -212,7 +233,9 @@
     for copy in t_copies:
         copy.start()
 
-    weights_in.wait()
+    for copy in other_copies:
+        copy.wait()
+    weight_copy.wait()
 
     def apply(left, right, op):
         w = wv[op]
@@ -230,7 +253,8 @@
     for side, base in ((0, 0), (1, RIM + tiles)):
         put_fluxes([halo[side, c] for c in range(comps)], base)
     neighbor_ids = lax.broadcasted_iota(jnp.int32, (tiles, tiles + 2 * RIM), 1)
-    shifted = adj[...] - (me_d * tiles - RIM)
+    shifted = jnp.concatenate([adj[...], jnp.zeros((8 - NEIGHBORS, tiles), jnp.int32)], axis=0)
+    shifted = shifted.T - (me_d * tiles - RIM)
     for direction in range(3):
         pick = jnp.concatenate(
             [
@@ -322,16 +346,25 @@
     wide = -(-comps // 2) * width
     packed = -(-(comps * slots) // 16) * 16
     in_vmem = pl.BlockSpec(memory_space=pltpu.VMEM)
-    in_smem = pl.BlockSpec(memory_space=pltpu.SMEM)
+    in_hbm = pl.BlockSpec(memory_space=pltpu.HBM)
+    i32 = jnp.int32
     bf16, f32 = jnp.bfloat16, jnp.float32
     dma = pltpu.SemaphoreType.DMA
     line = lambda values: values.reshape(1, faces)
     return pl.pallas_call(
         functools.partial(kernel, n, ndom, cells),
         out_shape=jax.ShapeDtypeStruct(flow_state.shape, f32),
-        in_specs=[in_vmem, pl.BlockSpec(memory_space=pl.ANY)] + [in_vmem] * 5 + [in_smem] * 2,
+        in_specs=[in_hbm] * 9,
         out_specs=in_vmem,
         scratch_shapes=[
+            pltpu.VMEM(flow_state.shape, f32),
+            pltpu.VMEM((NEIGHBORS, tiles), i32),
+            pltpu.VMEM((1, faces), i32),
+            pltpu.VMEM((1, faces), i32),
+            pltpu.VMEM((1, faces), i32),
+            pltpu.VMEM((1, faces), i32),
+            pltpu.SMEM((1,), i32),
+            pltpu.SMEM((1,), f32),
             pltpu.VMEM((n, rows, width), bf16),
             pltpu.VMEM((n, rows, width), bf16),
             pltpu.VMEM((n, rows, width), bf16),
@@ -345,7 +378,7 @@
             pltpu.VMEM((ndom, packed, faces), bf16),
             pltpu.VMEM((2, ndom, packed, faces), bf16),
             pltpu.VMEM((slots * tiles, wide), f32),
-            dma,
+            dma((9,)),
             dma((2, ndom)),
             dma((2, 2)),
             dma((2, n)),
@@ -353,10 +386,10 @@
             dma((2, 2, ndom)),
         ],
         compiler_params=pltpu.CompilerParams(
-            collective_id=0, has_side_effects=True, vmem_limit_bytes=40 * 1024 * 1024
+            collective_id=0, has_side_effects=True, vmem_limit_bytes=64 * 1024 * 1024
         ),
     )(
-        flow_state, op_weight, adjacency, line(face_tile), line(face_row),
+        flow_state, op_weight, adjacency.T, line(face_tile), line(face_row),
         line(face_partner), line(face_side), face_count, frequency,
     )
 

time: 25.2 us -> 20.8 us (0.83)
  local copies, waits for them, and re-layouts: 6.83 us -> 1.72 us
  Pallas kernels: 16.7 us -> 17.6 us
    unnamed x14 -> x1, local copies, waits for them, and re-layouts: 6.83 us -> 1.72 us
    pallas_call x1, Pallas kernels: 16.7 us -> 17.6 us  [body(): pl.pallas_call(functools.partial(kernel, n, ndom, cells), out_shape=jax.S...]
where the time goes in v2:
time: 20.8 us; the launch traced here: 20.7 us
  Pallas kernels  17.6 us (85%)
  local copies, waits for them, and re-layouts  1.72 us (8%)
  between operations  1.3 us (6%)
    pallas_call x1, Pallas kernels, body(): pl.pallas_call(functools.partial(kernel, n, ndom, cells), out_shape=jax.S...  17.6 us
    unnamed x1, local copies, waits for them, and re-layouts  1.72 us

profile of v2, /device:TPU:0, one launch (start us, length us, event | category | flops | bytes accessed | tf_op | source)
XLA Modules:
  0.0 20.7 jit_solution(9942163576180030200)
XLA Ops:
  1.3 17.6 %shard_map.91 = f32[5,128,128]{2,1,0:T(8,128)} custom-call(f32[5,128,128]{2,1,0:T(8,128)} %flow_in.1, bf16[9,320,320]{2,1,0:T(8,128)(2,1)} %weight.1, s32[6,128]{1,0:T(8,128)} %bitcast.5, s32[1,256]{1,0:T(1,128)} %bitcast.6, s32[1,256]{1,0:T(1,128)} %bitcast.7, s32[1,256]{1,0:T(1,128)} %bitcast.8, s32[1,256]{1,0:T(1,128)} %bitcast.9, s32[1]{0:T(128)S(6)} %copy.11.count_in, ...), custom_call_target="tpu_custom_call" | custom-call | tf_op jit(solution)/shard_map/pallas_call | solution.py:354
  18.9 1.7 %copy.13 = f32[5,128,128]{2,1,0:T(8,128)} copy(f32[5,128,128]{2,1,0:T(8,128)} %shard_map.91) | data formatting | bytes 655360

commit v3 on v2

--- a/solution.py
+++ b/solution.py
@@ -46,8 +46,8 @@
     flow_in, weight, adj_in, tile_in, row_in, partner_in, side_in, count_in, freq_in,
     out,
     flow, adj, face_tile, face_row, face_partner, face_side, count, freq,
-    ubf, ain, tout, tin, stage, halo, wv, fp, ut, codes, pout, pin, acc,
-    in_sem, code_sem, halo_sem, a_sem, t_sem, p_sem,
+    ubf, ain, tout, tin, stage, halo, wv, fp, ut, codes, pout, pmid, psum, pin, acc,
+    in_sem, code_sem, halo_sem, a_sem, t_sem, m_sem, p_sem,
 ):
     n, ndom = peers_inst, peers_dom
     comps, tiles, width = flow.shape
@@ -85,7 +85,7 @@
         )
 
     partners = {(j, 0) for j in range(1, ndom)} | {(0, i) for i in range(1, n)}
-    partners |= {(j, s % n) for j in range(ndom) for s in (lag, -lag)}
+    partners |= {(0, lag % n), (0, -lag % n)}
     partners = sorted(partners)
     barrier = pltpu.get_barrier_semaphore()
     for dom_step, inst_step in partners:
@@ -108,15 +108,12 @@
             )
         )
     ]
-    for copy in arriving:
+    for copy in arriving[:-1]:
         copy.start()
     flow_copy, partner_copy, row_copy, *other_copies, weight_copy = arriving
 
-    partner_copy.wait()
-    row_copy.wait()
-    code = face_partner[...] * cells + face_row[...]
-    codes[0] = jnp.broadcast_to(code, (8, faces))
     flow_copy.wait()
+    weight_copy.start()
     for p in range(n):
         if aligned:
             for c in range(comps):
@@ -128,6 +125,10 @@
             for c in range(comps):
                 stage[c * part : (c + 1) * part] = flow[c, p * part : (p + 1) * part]
             ubf[p] = stage[...].astype(jnp.bfloat16)
+    partner_copy.wait()
+    row_copy.wait()
+    code = face_partner[...] * cells + face_row[...]
+    codes[0] = jnp.broadcast_to(code, (8, faces))
     pl.semaphore_wait(barrier, len(partners))
 
     code_copies = [
@@ -135,11 +136,22 @@
     ]
     for copy in code_copies:
         copy.start()
+    halves = 2 if rows % (2 * CHUNK) == 0 else 1
+    half = rows // halves
     a_copies = [
-        remote(ubf.at[inst_at(i)], ain.at[i], a_sem, (i,), at(0, i)) for i in range(1, n)
+        [
+            remote(
+                ubf.at[inst_at(i), pl.ds(h * half, half)],
+                ain.at[i, pl.ds(h * half, half)],
+                a_sem, (i, h), at(0, i),
+            )
+            for i in range(1, n)
+        ]
+        for h in range(halves)
     ]
-    for copy in a_copies:
-        copy.start()
+    for group in a_copies:
+        for copy in group:
+            copy.start()
     halo_copies = [
         remote(flow_in.at[:, tiles - RIM :], halo.at[0], halo_sem, (0,), at(1, 0)),
         remote(flow_in.at[:, :RIM], halo.at[1], halo_sem, (1,), at(-1, 0)),
@@ -174,7 +186,7 @@
 
     cell_ids = lax.broadcasted_iota(jnp.int32, (cells, faces), 0)
     tile_ids = lax.broadcasted_iota(jnp.int32, (tiles, faces), 0)
-    p_copies = []
+    m_copies = []
     for j in range(ndom):
         if j:
             code_copies[j - 1].wait_recv()
@@ -193,14 +205,15 @@
             for g in range(comps * slots)
         ]
         lines.append(jnp.zeros((pout.shape[1] - comps * slots, faces), jnp.float32))
-        pout[j] = jnp.concatenate(lines, axis=0).astype(jnp.bfloat16)
-        for way, step in enumerate((-lag, lag)):
-            copy = remote(pout.at[j], pin.at[way, j], p_sem, (way, j), at(-j, step))
+        found = jnp.concatenate(lines, axis=0).astype(jnp.bfloat16)
+        if j == 0:
+            pmid[0] = found
+        else:
+            pout[j] = found
+            copy = remote(pout.at[j], pmid.at[j], m_sem, (j,), at(-j, 0))
             copy.start()
-            p_copies.append(copy)
-
-    for copy in a_copies:
-        copy.wait_recv()
+            m_copies.append(copy)
+
     cross = [
         jnp.where(
             low_lanes,
@@ -209,29 +222,53 @@
         ).astype(jnp.float32)
         for delta in range(n)
     ]
-    for r in range(0, rows, CHUNK):
-        plain = [
-            (ubf[me_i, r : r + CHUNK] if i == 0 else ain[i, r : r + CHUNK]).astype(jnp.float32)
-            for i in range(n)
+    t_copies = []
+    p_copies = []
+    for h in range(halves):
+        for copy in a_copies[h]:
+            copy.wait_recv()
+        for r in range(h * half, (h + 1) * half, CHUNK):
+            plain = [
+                (ubf[me_i, r : r + CHUNK] if i == 0 else ain[i, r : r + CHUNK]).astype(
+                    jnp.float32
+                )
+                for i in range(n)
+            ]
+            turned = [swap(value) for value in plain]
+            for m in range(n):
+                total = jnp.zeros((CHUNK, width), jnp.float32)
+                for i in range(n):
+                    even = derivative_entry(2 * (m + i), instances)
+                    if even != 0.0:
+                        total = total + even * plain[i]
+                    total = total + cross[(m + i) % n] * turned[i]
+                total = total.astype(jnp.bfloat16)
+                if m == 0:
+                    tin[me_i, r : r + CHUNK] = total
+                else:
+                    tout[m, r : r + CHUNK] = total
+        group = [
+            remote(
+                tout.at[m, pl.ds(h * half, half)],
+                tin.at[me_i, pl.ds(h * half, half)],
+                t_sem, (m, h), at(0, m),
+            )
+            for m in range(1, n)
         ]
-        turned = [swap(value) for value in plain]
-        for m in range(n):
-            total = jnp.zeros((CHUNK, width), jnp.float32)
-            for i in range(n):
-                even = derivative_entry(2 * (m + i), instances)
-                if even != 0.0:
-                    total = total + even * plain[i]
-                total = total + cross[(m + i) % n] * turned[i]
-            total = total.astype(jnp.bfloat16)
-            if m == 0:
-                tin[me_i, r : r + CHUNK] = total
-            else:
-                tout[m, r : r + CHUNK] = total
-    t_copies = [
-        remote(tout.at[m], tin.at[me_i], t_sem, (m,), at(0, m)) for m in range(1, n)
-    ]
-    for copy in t_copies:
-        copy.start()
+        for copy in group:
+            copy.start()
+        t_copies.append(group)
+        if h == 0:
+            for copy in m_copies:
+                copy.wait_recv()
+            known = pmid[0]
+            for j in range(1, ndom):
+                known = known + pmid[j]
+            psum[...] = known
+            for way, step in enumerate((-lag, lag)):
+                copy = remote(psum, pin.at[way], p_sem, (way,), at(0, step))
+                copy.start()
+                p_copies.append(copy)
 
     for copy in other_copies:
         copy.wait()
@@ -285,12 +322,7 @@
     )
     for copy in p_copies:
         copy.wait_recv()
-    upper = pin[0, 0].astype(jnp.float32)
-    lower = pin[1, 0].astype(jnp.float32)
-    for j in range(1, ndom):
-        upper = upper + pin[0, j].astype(jnp.float32)
-        lower = lower + pin[1, j].astype(jnp.float32)
-    lagged = jnp.where(side, upper, lower)
+    lagged = jnp.where(side, pin[0].astype(jnp.float32), pin[1].astype(jnp.float32))
     lines = [lagged[g : g + 1] for g in range(comps * slots)]
     cosine = math.cos(2.0 * math.pi / BLADES)
     sine = jnp.where(side, 1.0, -1.0) * math.sin(2.0 * math.pi / BLADES)
@@ -303,32 +335,40 @@
     )
     gained = lax.dot_general(place, spread, contract, preferred_element_type=jnp.float32)
 
-    for copy in t_copies:
-        copy.wait_recv()
-    speed = freq[0]
-    low = lax.broadcasted_iota(jnp.int32, (part, width), 1) < cells
-    for p in range(n):
-        span = slice(p * part, (p + 1) * part)
-        more = slice(tiles + p * part, tiles + (p + 1) * part)
-        if not aligned:
-            stage[...] = tin[p].astype(jnp.float32)
+    for t in range(0, tiles, CHUNK):
+        span = slice(t, t + CHUNK)
+        more = slice(tiles + t, tiles + t + CHUNK)
         for c in range(comps):
             pair = c // 2
             cols = slice(pair * width, (pair + 1) * width)
             if c % 2 == 0:
-                spatial = jnp.where(low, acc[span, cols], swap(acc[more, cols]))
+                spatial = jnp.where(low_lanes, acc[span, cols], swap(acc[more, cols]))
             else:
-                spatial = jnp.where(low, swap(acc[span, cols]), acc[more, cols])
+                spatial = jnp.where(low_lanes, swap(acc[span, cols]), acc[more, cols])
+            out[c, span] = (
+                spatial
+                + gained[span, c * width : (c + 1) * width]
+                - times[span] * flow[c, span]
+            )
+    speed = freq[0]
+    for m in range(n):
+        if m:
+            for group in t_copies:
+                group[m - 1].wait_recv()
+        p = inst_at(-m)
+        if not aligned:
+            stage[...] = tin[p].astype(jnp.float32)
+        for c in range(comps):
             block = slice(c * part, (c + 1) * part)
             temporal = tin[p, block].astype(jnp.float32) if aligned else stage[block]
-            out[c, span] = (
-                spatial
-                + speed * temporal
-                + gained[span, c * width : (c + 1) * width]
-                - times[span] * flow[c, span]
-            )
-
-    for copy in code_copies + a_copies + halo_copies + p_copies + t_copies:
+            if aligned:
+                span = pl.ds(pl.multiple_of(p * part, part), part)
+            else:
+                span = pl.ds(p * part, part)
+            out[c, span] = out[c, span] + speed * temporal
+
+    flat = [copy for group in a_copies + t_copies for copy in group]
+    for copy in code_copies + flat + halo_copies + m_copies + p_copies:
         copy.wait_send()
 
 
@@ -376,14 +416,17 @@
             pltpu.VMEM((comps * width, tiles), bf16),
             pltpu.VMEM((ndom, 8, faces), jnp.int32),
             pltpu.VMEM((ndom, packed, faces), bf16),
-            pltpu.VMEM((2, ndom, packed, faces), bf16),
+            pltpu.VMEM((ndom, packed, faces), bf16),
+            pltpu.VMEM((packed, faces), bf16),
+            pltpu.VMEM((2, packed, faces), bf16),
             pltpu.VMEM((slots * tiles, wide), f32),
             dma((9,)),
             dma((2, ndom)),
             dma((2, 2)),
-            dma((2, n)),
-            dma((2, n)),
-            dma((2, 2, ndom)),
+            dma((2, n, 2)),
+            dma((2, n, 2)),
+            dma((2, ndom)),
+            dma((2, 2)),
         ],
         compiler_params=pltpu.CompilerParams(
             collective_id=0, has_side_effects=True, vmem_limit_bytes=64 * 1024 * 1024

time: 20.8 us -> 19.2 us (0.923)
  Pallas kernels: 17.6 us -> 16 us
    pallas_call x1, Pallas kernels: 17.6 us -> 16 us  [body(): pl.pallas_call(functools.partial(kernel, n, ndom, cells), out_shape=jax.S...]
where the time goes in v3:
time: 19.2 us; the launch traced here: 19 us
  Pallas kernels  16 us (83%)
  local copies, waits for them, and re-layouts  1.72 us (9%)
  between operations  1.3 us (7%)
    pallas_call x1, Pallas kernels, body(): pl.pallas_call(functools.partial(kernel, n, ndom, cells), out_shape=jax.S...  16 us
    unnamed x1, local copies, waits for them, and re-layouts  1.72 us

profile of v3, /device:TPU:0, one launch (start us, length us, event | category | flops | bytes accessed | tf_op | source)
XLA Modules:
  0.0 19.0 jit_solution(2851325112797723059)
XLA Ops:
  1.3 16.0 %shard_map.91 = f32[5,128,128]{2,1,0:T(8,128)} custom-call(f32[5,128,128]{2,1,0:T(8,128)} %flow_in.1, bf16[9,320,320]{2,1,0:T(8,128)(2,1)} %weight.1, s32[6,128]{1,0:T(8,128)} %bitcast.5, s32[1,256]{1,0:T(1,128)} %bitcast.6, s32[1,256]{1,0:T(1,128)} %bitcast.7, s32[1,256]{1,0:T(1,128)} %bitcast.8, s32[1,256]{1,0:T(1,128)} %bitcast.9, s32[1]{0:T(128)S(6)} %copy.11.count_in, ...), custom_call_target="tpu_custom_call" | custom-call | tf_op jit(solution)/shard_map/pallas_call | solution.py:394
  17.3 1.7 %copy.13 = f32[5,128,128]{2,1,0:T(8,128)} copy(f32[5,128,128]{2,1,0:T(8,128)} %shard_map.91) | data formatting | bytes 655360

commit v4 on v3

--- a/solution.py
+++ b/solution.py
@@ -43,11 +43,11 @@
 
 def kernel(
     peers_inst, peers_dom, cells,
-    flow_in, weight, adj_in, tile_in, row_in, partner_in, side_in, count_in, freq_in,
-    out,
-    flow, adj, face_tile, face_row, face_partner, face_side, count, freq,
-    ubf, ain, tout, tin, stage, halo, wv, fp, ut, codes, pout, pmid, psum, pin, acc,
-    in_sem, code_sem, halo_sem, a_sem, t_sem, m_sem, p_sem,
+    flow_in, weight, adj_in, tile_in, row_in, partner_in, side_in, count_in,
+    base_out, tin,
+    flow, adj, face_tile, face_row, face_partner, face_side, count,
+    out, ubf, ain, tout, stage, halo, wv, fp, ut, codes, pout, pmid, psum, pin, acc,
+    in_sem, code_sem, halo_sem, a_sem, t_sem, m_sem, p_sem, out_sem,
 ):
     n, ndom = peers_inst, peers_dom
     comps, tiles, width = flow.shape
@@ -103,7 +103,6 @@
                 (tile_in, face_tile),
                 (side_in, face_side),
                 (count_in, count),
-                (freq_in, freq),
                 (weight, wv),
             )
         )
@@ -224,6 +223,7 @@
     ]
     t_copies = []
     p_copies = []
+    leaving = []
     for h in range(halves):
         for copy in a_copies[h]:
             copy.wait_recv()
@@ -243,10 +243,7 @@
                         total = total + even * plain[i]
                     total = total + cross[(m + i) % n] * turned[i]
                 total = total.astype(jnp.bfloat16)
-                if m == 0:
-                    tin[me_i, r : r + CHUNK] = total
-                else:
-                    tout[m, r : r + CHUNK] = total
+                tout[m, r : r + CHUNK] = total
         group = [
             remote(
                 tout.at[m, pl.ds(h * half, half)],
@@ -258,6 +255,13 @@
         for copy in group:
             copy.start()
         t_copies.append(group)
+        own_copy = pltpu.make_async_copy(
+            tout.at[0, pl.ds(h * half, half)],
+            tin.at[me_i, pl.ds(h * half, half)],
+            out_sem.at[1 + h],
+        )
+        own_copy.start()
+        leaving.append(own_copy)
         if h == 0:
             for copy in m_copies:
                 copy.wait_recv()
@@ -350,26 +354,50 @@
                 + gained[span, c * width : (c + 1) * width]
                 - times[span] * flow[c, span]
             )
-    speed = freq[0]
-    for m in range(n):
-        if m:
-            for group in t_copies:
-                group[m - 1].wait_recv()
-        p = inst_at(-m)
-        if not aligned:
-            stage[...] = tin[p].astype(jnp.float32)
-        for c in range(comps):
-            block = slice(c * part, (c + 1) * part)
-            temporal = tin[p, block].astype(jnp.float32) if aligned else stage[block]
-            if aligned:
-                span = pl.ds(pl.multiple_of(p * part, part), part)
-            else:
-                span = pl.ds(p * part, part)
-            out[c, span] = out[c, span] + speed * temporal
+    base_copy = pltpu.make_async_copy(out, base_out, out_sem.at[0])
+    base_copy.start()
+    for group in t_copies:
+        for copy in group:
+            copy.wait_recv()
+    for copy in leaving + [base_copy]:
+        copy.wait()
 
     flat = [copy for group in a_copies + t_copies for copy in group]
     for copy in code_copies + flat + halo_copies + m_copies + p_copies:
         copy.wait_send()
+
+
+def finish(base_in, tin_in, freq, out, base, tin, stage, sems):
+    comps, tiles, _ = base.shape
+    n, _, _ = tin.shape
+    part = tiles // n
+    aligned = part % CHUNK == 0
+    tin_copy = pltpu.make_async_copy(tin_in, tin, sems.at[2 * comps])
+    tin_copy.start()
+    copies = [
+        pltpu.make_async_copy(base_in.at[c], base.at[c], sems.at[c]) for c in range(comps)
+    ]
+    for copy in copies:
+        copy.start()
+    leaving = [
+        pltpu.make_async_copy(base.at[c], out.at[c], sems.at[comps + c]) for c in range(comps)
+    ]
+    tin_copy.wait()
+    speed = freq[0]
+    for c in range(comps):
+        copies[c].wait()
+        for p in range(n):
+            span = slice(p * part, (p + 1) * part)
+            block = slice(c * part, (c + 1) * part)
+            if aligned:
+                temporal = tin[p, block].astype(jnp.float32)
+            else:
+                stage[...] = tin[p].astype(jnp.float32)
+                temporal = stage[block]
+            base[c, span] = base[c, span] + speed * temporal
+        leaving[c].start()
+    for copy in leaving:
+        copy.wait()
 
 
 def body(
@@ -385,17 +413,20 @@
     rows = -(-(comps * (tiles // n)) // CHUNK) * CHUNK
     wide = -(-comps // 2) * width
     packed = -(-(comps * slots) // 16) * 16
-    in_vmem = pl.BlockSpec(memory_space=pltpu.VMEM)
     in_hbm = pl.BlockSpec(memory_space=pltpu.HBM)
     i32 = jnp.int32
     bf16, f32 = jnp.bfloat16, jnp.float32
     dma = pltpu.SemaphoreType.DMA
     line = lambda values: values.reshape(1, faces)
-    return pl.pallas_call(
+    derived = (n, rows, width)
+    base, tin = pl.pallas_call(
         functools.partial(kernel, n, ndom, cells),
-        out_shape=jax.ShapeDtypeStruct(flow_state.shape, f32),
-        in_specs=[in_hbm] * 9,
-        out_specs=in_vmem,
+        out_shape=(
+            jax.ShapeDtypeStruct(flow_state.shape, f32),
+            jax.ShapeDtypeStruct(derived, bf16),
+        ),
+        in_specs=[in_hbm] * 8,
+        out_specs=(in_hbm, in_hbm),
         scratch_shapes=[
             pltpu.VMEM(flow_state.shape, f32),
             pltpu.VMEM((NEIGHBORS, tiles), i32),
@@ -404,11 +435,10 @@
             pltpu.VMEM((1, faces), i32),
             pltpu.VMEM((1, faces), i32),
             pltpu.SMEM((1,), i32),
-            pltpu.SMEM((1,), f32),
-            pltpu.VMEM((n, rows, width), bf16),
-            pltpu.VMEM((n, rows, width), bf16),
-            pltpu.VMEM((n, rows, width), bf16),
-            pltpu.VMEM((n, rows, width), bf16),
+            pltpu.VMEM(flow_state.shape, f32),
+            pltpu.VMEM(derived, bf16),
+            pltpu.VMEM(derived, bf16),
+            pltpu.VMEM(derived, bf16),
             pltpu.VMEM((rows, width), f32),
             pltpu.VMEM((2, comps, RIM, width), f32),
             pltpu.VMEM(op_weight.shape, bf16),
@@ -420,21 +450,35 @@
             pltpu.VMEM((packed, faces), bf16),
             pltpu.VMEM((2, packed, faces), bf16),
             pltpu.VMEM((slots * tiles, wide), f32),
-            dma((9,)),
+            dma((8,)),
             dma((2, ndom)),
             dma((2, 2)),
             dma((2, n, 2)),
             dma((2, n, 2)),
             dma((2, ndom)),
             dma((2, 2)),
+            dma((3,)),
         ],
         compiler_params=pltpu.CompilerParams(
             collective_id=0, has_side_effects=True, vmem_limit_bytes=64 * 1024 * 1024
         ),
     )(
         flow_state, op_weight, adjacency.T, line(face_tile), line(face_row),
-        line(face_partner), line(face_side), face_count, frequency,
+        line(face_partner), line(face_side), face_count,
     )
+    return pl.pallas_call(
+        finish,
+        out_shape=jax.ShapeDtypeStruct(base.shape, f32),
+        in_specs=[in_hbm, in_hbm, pl.BlockSpec(memory_space=pltpu.SMEM)],
+        out_specs=in_hbm,
+        scratch_shapes=[
+            pltpu.VMEM(base.shape, f32),
+            pltpu.VMEM(derived, bf16),
+            pltpu.VMEM((rows, width), f32),
+            dma((2 * comps + 1,)),
+        ],
+        compiler_params=pltpu.CompilerParams(vmem_limit_bytes=64 * 1024 * 1024),
+    )(base, tin, frequency)
 
 
 def solution(mesh):

time: 19.2 us -> 19.2 us (level)
  local copies, waits for them, and re-layouts: 1.72 us -> 0 us
  Pallas kernels: 16 us -> 17.7 us
    pallas_call x1 -> x2, Pallas kernels: 16 us -> 17.7 us  [the longest x1 15.9 us: body(): pl.pallas_call(functools.partial(kernel, n, ndom, cells), out_shape=(jax....]
    unnamed x1 -> x0, local copies, waits for them, and re-layouts: 1.72 us -> none
where the time goes in v4:
time: 19.2 us; the launch traced here: 19 us
  Pallas kernels  17.7 us (92%)
  between operations  1.31 us (7%)
    pallas_call x1, Pallas kernels, body(): pl.pallas_call(functools.partial(kernel, n, ndom, cells), out_shape=(jax....  15.9 us
    pallas_call x1, Pallas kernels, body(): pl.pallas_call(finish, out_shape=jax.ShapeDtypeStruct(base.shape, f32), i...  1.78 us

profile of v4, /device:TPU:0, one launch (start us, length us, event | category | flops | bytes accessed | tf_op | source)
XLA Modules:
  0.0 19.0 jit_solution(4668937948090249062)
XLA Ops:
  1.3 15.9 %shard_map.91 = (f32[5,128,128]{2,1,0:T(8,128)}, bf16[4,160,128]{2,1,0:T(8,128)(2,1)}) custom-call(f32[5,128,128]{2,1,0:T(8,128)} %flow_in.1, bf16[9,320,320]{2,1,0:T(8,128)(2,1)} %weight.1, s32[6,128]{1,0:T(8,128)} %bitcast.5, s32[1,256]{1,0:T(1,128)} %bitcast.6, s32[1,256]{1,0:T(1,128)} %bitcast.7, s32[1,256]{1,0:T(1,128)} %bitcast.8, s32[1,256]{1,0:T(1,128)} %bitcast.9, ...), custom_call_target="tpu_custom_call" | custom-call | tf_op jit(solution)/shard_map/pallas_call | solution.py:422
  17.2 1.8 %shard_map.92 = f32[5,128,128]{2,1,0:T(8,128)} custom-call(f32[5,128,128]{2,1,0:T(8,128)} %get-tuple-element.7.base_in, bf16[4,160,128]{2,1,0:T(8,128)(2,1)} %get-tuple-element.8.tin_in, f32[1]{0:T(128)S(6)} %copy.11.freq), custom_call_target="tpu_custom_call" | custom-call | tf_op jit(solution)/shard_map/pallas_call | solution.py:469
